TPU v7x, 32 devices: a whole 2x2x4 slice. The times are simulated.
32 devices in a mesh: groups: 2 (over x), slab: 16 (over z, y, core).
Axes of the slice: x: 2, y: 2, z: 4, core: 2. Of those that a mesh axis runs over, the one named last changes fastest.
Arguments:
- atomic_descriptors: float32 [98304, 128], P(('groups', 'slab')), parts along dimension 0, may hold values from -80 to 80
- fractional_locations: float32 [3, 98304], P(None, ('groups', 'slab')), parts along dimension 1, may hold values from 0 to 1
- filled_slot_tallies: int32 [32], P(('groups', 'slab')), parts along dimension 0, may hold values from 0 to 3072, as said below
- reciprocal_lattice_indices: int32 [3, 1024], replicated, may hold values from -8 to 8
- spectral_kernels: float32 [2, 1024, 128], replicated, may hold values from -0.1875 to 0.1875
- initial_mixing_matrix: float32 [2, 128, 128], replicated, may hold values from -0.5 to 0.5
- closing_mixing_matrix: float32 [2, 128, 128], replicated, may hold values from -0.5 to 0.5
Outputs:
- features_out: float32 [98304, 128], P(('groups', 'slab')), parts along dimension 0
There are 2 independent parts, one for each index of `groups`. A program takes and returns all parts, laid end to end along the dimension named above; an argument that names none is the same for every part. Nothing has to cross between parts.
Inputs may be any that keep to these rules, and one draw needn't show every extreme that they name: Write b(i) for filled_slot_tallies[i] / 128 rounded up. For every i < 8: b(i) + b(i + 8) <= 24, with equality for i = 7.
All inputs are finite; a program needn't handle non-finite values.
Results may differ from a plain program's by a relative error of at most 0.0003.
Values sent between devices are 32-bit elements; how exact they have to be, the bound alone decides.
A program may use at most 64 MiB of HBM per device.

v0:
```python
import functools
import math

import jax
import jax.numpy as jnp
from jax import lax
from jax.experimental import pallas as pl
from jax.experimental.pallas import tpu as pltpu
from jax.sharding import PartitionSpec as P
import numpy as np

TILE = 256
HALF_TURN_SPAN = 0.5


def fit_half_angle():
    nodes = np.cos((np.arange(400) + 0.5) * np.pi / 400) * HALF_TURN_SPAN
    square = nodes * nodes
    root = math.sqrt(2.0)
    odd = np.stack([nodes * square**i for i in range(5)], 1)
    even = np.stack([square**i for i in range(5)], 1)
    sin_fit = np.linalg.lstsq(odd, root * np.sin(np.pi * nodes), rcond=None)[0]
    cos_fit = np.linalg.lstsq(even, root * np.cos(np.pi * nodes), rcond=None)[0]
    return [float(v) for v in sin_fit], [float(v) for v in cos_fit]


SIN_FIT, COS_FIT = fit_half_angle()


def horner(square, coefs):
    value = coefs[-1] * square + coefs[-2]
    for coef in coefs[-3::-1]:
        value = value * square + coef
    return value


def split(value):
    high = value.astype(jnp.bfloat16)
    return high, (value - high.astype(jnp.float32)).astype(jnp.bfloat16)


def cos_sin_turns(turns):
    magic = 12582912.0
    rest = turns - ((turns + magic) - magic)
    square = rest * rest
    s = rest * horner(square, SIN_FIT)
    c = horner(square, COS_FIT)
    return 1.0 - s * s, s * c


def dot(a, b, dims):
    return lax.dot_general(a, b, (dims, ((), ())), preferred_element_type=jnp.float32)


def dot_hp(a, b):
    return lax.dot_general(
        a, b, (((1,), (0,)), ((), ())),
        precision=lax.Precision.HIGHEST, preferred_element_type=jnp.float32,
    )


NN = ((1,), (0,))
NT = ((1,), (1,))
TN = ((0,), (0,))


def occupied_row(tally, first, width):
    return (first + lax.broadcasted_iota(jnp.int32, (1, width), 1) < tally).astype(jnp.float32)


def coordinate_parts(coords):
    high = coords.astype(jnp.bfloat16).astype(jnp.float32)
    rest = coords - high
    mid = rest.astype(jnp.bfloat16).astype(jnp.float32)
    low = rest - mid
    return jnp.concatenate([high, mid, low, jnp.zeros_like(low)], axis=0).astype(jnp.bfloat16)


def update(states_t, high, low, w_high, w_low, first_t, second_t):
    c = w_high.shape[0]
    both = dot(jnp.concatenate([w_high, w_low], 0), high, NT)
    potential = both[:c] + both[c:] + dot(w_high, low, NT)
    v = dot_hp(first_t, potential)
    return states_t + dot_hp(second_t, v / (1.0 + jnp.exp(-v)))


def first_kernel(tally, states, coords, k_parts, high_out, low_out, s_out, density_out, charge_out):
    i = pl.program_id(0)
    kspace = k_parts.shape[1]
    c = states.shape[1]
    occ = occupied_row(tally[0], i * TILE, TILE)
    weighted = states[...].T * occ
    w_high, w_low = split(weighted)
    occ16 = jnp.broadcast_to(occ, (16, TILE)).astype(jnp.bfloat16)
    lhs_high = jnp.concatenate([w_high, w_low, occ16], 0)
    lhs_low = jnp.concatenate([w_high, occ16], 0)
    parts = coordinate_parts(coords[...])

    @pl.when(i == 0)
    def _():
        s_out[...] = jnp.zeros_like(s_out)
        density_out[...] = jnp.zeros_like(density_out)
        charge_out[...] = jnp.zeros_like(charge_out)

    charge_out[...] += jnp.broadcast_to(jnp.sum(weighted, axis=1, keepdims=True), charge_out.shape)
    step = 256
    for k in range(0, kspace, step):
        turns = dot(parts, k_parts[:, k : k + step], TN)
        for value, at in zip(cos_sin_turns(turns), (k, kspace + k)):
            high, low = split(value)
            high_out[:, at : at + step] = high
            low_out[:, at : at + step] = low
            one = dot(lhs_high, high, NN)
            two = dot(lhs_low, low, NN)
            s_out[:, at : at + step] += one[:c] + one[c : 2 * c] + two[:c]
            density_out[:, at : at + step] += (one[2 * c :] + two[c:])[:8]


def middle_kernel(tally, states, high, low, w_high, w_low, first_t, second_t, fresh_out, s_out, charge_out):
    i = pl.program_id(0)
    c = states.shape[1]
    occ = occupied_row(tally[0], i * TILE, TILE)

    @pl.when(i == 0)
    def _():
        s_out[...] = jnp.zeros_like(s_out)
        charge_out[...] = jnp.zeros_like(charge_out)

    fresh = update(
        states[...].T, high[...], low[...], w_high[...], w_low[...], first_t[...], second_t[...]
    )
    fresh_out[...] = fresh
    weighted = fresh * occ
    charge_out[...] += jnp.broadcast_to(jnp.sum(weighted, axis=1, keepdims=True), charge_out.shape)
    x_high, x_low = split(weighted)
    one = dot(jnp.concatenate([x_high, x_low], 0), high[...], NN)
    s_out[...] += one[:c] + one[c:] + dot(x_high, low[...], NN)


def last_kernel(tally, states_t, high, low, w_high, w_low, first_t, second_t, out):
    i = pl.program_id(0)
    occ = occupied_row(tally[0], i * TILE, TILE)
    fresh = update(
        states_t[...], high[...], low[...], w_high[...], w_low[...], first_t[...], second_t[...]
    )
    out[...] = (fresh * occ).T


def body(states, coords, tallies, lattice, kernels, first_matrix, second_matrix):
    slots, c = states.shape
    kspace = lattice.shape[1]
    width = 2 * kspace
    grid = (slots // TILE,)
    f32, b16 = jnp.float32, jnp.bfloat16
    shape = jax.ShapeDtypeStruct
    coords8 = jnp.pad(coords, ((0, 5), (0, 0)))
    k8 = jnp.pad(lattice, ((0, 5), (0, 0))).astype(b16)
    k_parts = jnp.concatenate([k8, k8, k8, k8], 0)
    first_t = jnp.swapaxes(first_matrix, 1, 2)
    second_t = jnp.swapaxes(second_matrix, 1, 2)
    kernels_t = jnp.swapaxes(kernels, 1, 2)

    tally_spec = pl.BlockSpec(memory_space=pltpu.SMEM)
    rows = lambda n: pl.BlockSpec((TILE, n), lambda i: (i, 0))
    lanes = lambda n: pl.BlockSpec((n, TILE), lambda i: (0, i))
    whole = lambda *s: pl.BlockSpec(s, lambda i: (0,) * len(s))
    params = pltpu.CompilerParams(vmem_limit_bytes=60 * 2**20)

    high, low, s, density, charge = pl.pallas_call(
        first_kernel,
        grid=grid,
        in_specs=[tally_spec, rows(c), lanes(8), whole(32, kspace)],
        out_specs=[rows(width), rows(width), whole(c, width), whole(8, width), whole(c, 128)],
        out_shape=[
            shape((slots, width), b16), shape((slots, width), b16),
            shape((c, width), f32), shape((8, width), f32), shape((c, 128), f32),
        ],
        compiler_params=params,
    )(tallies, states, coords8, k_parts)

    total = tallies[0].astype(f32)
    s, density, charge, total = lax.psum((s, density[:1], charge[:, :1], total), "slab")

    def weights(s, charge, kernel_t):
        w = (s - (charge / total) * density) / jnp.sqrt(total) * jnp.concatenate([kernel_t, kernel_t], 1)
        w_high = lax.reduce_precision(w, 8, 7)
        return w_high.astype(b16), (w - w_high).astype(b16)

    w_high, w_low = weights(s, charge, kernels_t[0])
    common = [rows(width), rows(width), whole(c, width), whole(c, width), whole(c, c), whole(c, c)]
    fresh, s, charge = pl.pallas_call(
        middle_kernel,
        grid=grid,
        in_specs=[tally_spec, rows(c)] + common,
        out_specs=[lanes(c), whole(c, width), whole(c, 128)],
        out_shape=[shape((c, slots), f32), shape((c, width), f32), shape((c, 128), f32)],
        compiler_params=params,
    )(tallies, states, high, low, w_high, w_low, first_t[0], second_t[0])
    s, charge = lax.psum((s, charge[:, :1]), "slab")
    w_high, w_low = weights(s, charge, kernels_t[1])
    return pl.pallas_call(
        last_kernel,
        grid=grid,
        in_specs=[tally_spec, lanes(c)] + common,
        out_specs=rows(c),
        out_shape=shape((slots, c), f32),
        compiler_params=params,
    )(tallies, fresh, high, low, w_high, w_low, first_t[1], second_t[1])


def solution(mesh):
    in_specs = (
        P(("groups", "slab"), None),
        P(None, ("groups", "slab")),
        P(("groups", "slab")),
        P(),
        P(),
        P(),
        P(),
    )
    out_specs = P(("groups", "slab"), None)
    return jax.shard_map(body, mesh=mesh, in_specs=in_specs, out_specs=out_specs, check_vma=False)
```

profile of v0, /device:TPU:0, one launch (start us, length us, event | category | flops | bytes accessed | tf_op | source)
XLA Modules:
  0.0 301.9 jit_solution(9687157733535143891)
XLA Ops:
  6.5 0.0 all-reduce.6.cloned.1.call-start
  7.2 0.7 convert.4
  7.9 0.6 pad_maximum_fusion.k_parts
  8.5 0.0 copy-start.1
  8.5 1.5 pad.9.coords
  10.0 0.0 copy-start.2
  10.0 0.0 copy-start
  10.0 29.6 %shard_map.73 = (bf16[3072,2048]{1,0:T(8,128)(2,1)}, bf16[3072,2048]{1,0:T(8,128)(2,1)}, f32[128,2048]{1,0:T(8,128)}, f32[8,2048]{1,0:T(8,128)}, f32[128,128]{1,0:T(8,128)}) custom-call(s32[1]{0:T(128)S(6)} %copy.16.tally, f32[3072,128]{1,0:T(8,128)} %states.3, f32[8,3072]{1,0:T(8,128)} %pad.9.coords, bf16[32,1024]{1,0:T(8,128)(2,1)} %pad_maximum_fusion.k_parts), custom_call_target="tpu_custom_call" | custom-call | tf_op jit(solution)/shard_map/pallas_call | solution.py:169
  39.7 0.0 all-reduce.6.cloned.1.call-update
  39.7 0.0 all-reduce.8.cloned.1.call-start
  39.7 0.8 slice.28
  40.6 65.7 %all-reduce.2 = (f32[]{:T(128)}, f32[2048]{0:T(1024)S(1)}, f32[128,1]{1,0:T(8,128)S(1)}) all-reduce(f32[]{:T(128)} %bitcast, f32[2048]{0:T(1024)S(1)} %bitcast.24, f32[128,1]{1,0:T(8,128)} %bitcast.22), channel_id=1, replica_groups=mesh['groups'=2,'slab'=16] {'slab'}, use_global_device_ids=true, to_apply=%region_2.3 | all-reduce | flops 2177 | bytes 17416 | tf_op jit(solution)/shard_map/psum | solution.py:182
  106.3 0.7 divide_reduce_fusion.1
  107.7 0.0 copy-done.1
  107.7 0.1 copy.12
  107.8 0.0 copy-done.2
  107.8 0.1 copy.13
  107.9 0.0 copy-done
  107.9 0.3 copy.11
  108.3 0.7 slice_bitcast_fusion.2
  109.0 0.1 slice_bitcast_fusion
  109.1 26.8 %all-reduce.6.cloned.1.call-done = f32[128,2048]{1,0:T(8,128)} async-done(((f32[128,2048]{1,0:T(8,128)}), f32[128,2048]{1,0:T(8,128)}) %all-reduce.6.cloned.1.call-update) | async-done | bytes 1048592 | tf_op jit(solution)/shard_map/psum | solution.py:182
  135.9 2.3 fusion
  138.2 0.9 reduce-precision_convert_fusion.1.w_high
  139.1 36.9 %shard_map.74 = (f32[128,3072]{1,0:T(8,128)}, f32[128,2048]{1,0:T(8,128)}, f32[128,128]{1,0:T(8,128)}) custom-call(s32[1]{0:T(128)S(6)} %copy.16.tally, f32[3072,128]{1,0:T(8,128)} %states.3, bf16[3072,2048]{1,0:T(8,128)(2,1)} %get-tuple-element.13.high, bf16[3072,2048]{1,0:T(8,128)(2,1)} %get-tuple-element.14.low, ...), custom_call_target="tpu_custom_call" | custom-call | tf_op jit(solution)/shard_map/pallas_call | solution.py:191
  176.0 0.0 all-reduce.8.cloned.1.call-update
  176.0 59.5 %psum.47 = f32[128,1]{1,0:T(8,128)S(1)} all-reduce(f32[128,1]{1,0:T(8,128)} %bitcast.23), channel_id=1, replica_groups=mesh['groups'=2,'slab'=16] {'slab'}, use_global_device_ids=true, to_apply=%region_5.6 | all-reduce | flops 128 | bytes 1024 | tf_op jit(solution)/shard_map/psum | solution.py:199
  235.5 0.7 divide_reduce_fusion
  236.2 32.5 %all-reduce.8.cloned.1.call-done = f32[128,2048]{1,0:T(8,128)} async-done(((f32[128,2048]{1,0:T(8,128)}), f32[128,2048]{1,0:T(8,128)}) %all-reduce.8.cloned.1.call-update) | async-done | bytes 1048592 | tf_op jit(solution)/shard_map/psum | solution.py:199
  268.7 2.3 fusion.1
  271.1 0.8 reduce-precision_convert_fusion.w_high
  271.9 23.1 %shard_map.75 = f32[3072,128]{1,0:T(8,128)} custom-call(s32[1]{0:T(128)S(6)} %copy.16.tally, f32[128,3072]{1,0:T(8,128)} %get-tuple-element.18.states_t, bf16[3072,2048]{1,0:T(8,128)(2,1)} %get-tuple-element.13.high, bf16[3072,2048]{1,0:T(8,128)(2,1)} %get-tuple-element.14.low, bf16[128,2048]{1,0:T(8,128)(2,1)} %reduce-precision_convert_fusion.w_high, ...), custom_call_target="tpu_custom_call" | custom-call | tf_op jit(solution)/shard_map/pallas_call | solution.py:201
  (1 shorter events, 0.0 us)
Async XLA Ops:
  6.5 129.3 %all-reduce.6.cloned.1.call-start = ((), (), s32[]{:S(2)}) async-start(), calls=%async_computation | async-start | bytes 2097152 | tf_op jit(solution)/shard_map/psum | solution.py:182
  8.5 99.2 %copy-start.1 = (f32[2,128,128]{2,1,0:T(8,128)S(1)}, f32[2,128,128]{2,1,0:T(8,128)}, u32[]{:S(2)}) copy-start(f32[2,128,128]{2,1,0:T(8,128)} %param.12) | copy-start | bytes 393220
  10.0 97.8 %copy-start.2 = (f32[2,128,128]{2,1,0:T(8,128)S(1)}, f32[2,128,128]{2,1,0:T(8,128)}, u32[]{:S(2)}) copy-start(f32[2,128,128]{2,1,0:T(8,128)} %param.13) | copy-start | bytes 393220
  10.0 97.9 %copy-start = (f32[2,1024,128]{2,1,0:T(8,128)S(1)}, f32[2,1024,128]{2,1,0:T(8,128)}, u32[]{:S(2)}) copy-start(f32[2,1024,128]{2,1,0:T(8,128)} %param.11) | copy-start | bytes 3145732
  39.7 229.0 %all-reduce.8.cloned.1.call-start = ((), (), s32[]{:S(2)}) async-start(), calls=%async_computation.1 | async-start | bytes 2097152 | tf_op jit(solution)/shard_map/psum | solution.py:199
Sparse Core Ops, SparseCore 0:
  39.8 96.0 all-reduce.5
  176.1 92.5 all-reduce.7
where the time goes:
time: 302 us
  blocking collectives  125 us (41%)
  Pallas kernels  89.6 us (30%)
  waiting for transfers between devices  59.3 us (20%)
  between operations  14.8 us (5%)
  other arithmetic  9.23 us (3%)
  local copies, waits for them, and re-layouts  3.7 us (1%)
    psum x1, blocking collectives, body(): lax.psum((s, density[:1], charge[:, :1], total), 'slab')  65.7 us
    psum x1, blocking collectives, body(): s, charge = lax.psum((s, charge[:, :1]), 'slab')  59.5 us
    pallas_call x1, Pallas kernels, body(): pl.pallas_call(middle_kernel, grid=grid, in_specs=[tally_spec, rows(c)] +...  36.9 us
    psum x1, waiting for transfers between devices, body(): s, charge = lax.psum((s, charge[:, :1]), 'slab')  32.5 us
    pallas_call x1, Pallas kernels, body(): pl.pallas_call(first_kernel, grid=grid, in_specs=[tally_spec, rows(c), la...  29.6 us
    psum x1, waiting for transfers between devices, body(): lax.psum((s, density[:1], charge[:, :1], total), 'slab')  26.8 us
    pallas_call x1, Pallas kernels, body(): pl.pallas_call(last_kernel, grid=grid, in_specs=[tally_spec, lanes(c)] +...  23.1 us
    convert_element_type x4, other arithmetic, weights(): return (w_high.astype(b16), (w - w_high).astype(b16))  6.41 us
  transfers between devices with their start and end apart: 2, of which 2 were waited for; matrix products, arithmetic and copies ran while one was open for 1% of the time, Pallas kernels for 0%

commit v1 on v0

v1 whole, which is shorter than its diff:
```python
import functools
import math

import jax
import jax.numpy as jnp
from jax import lax
from jax.experimental import pallas as pl
from jax.experimental.pallas import tpu as pltpu
from jax.sharding import PartitionSpec as P
import numpy as np

TILE = 512
PIECES = 3
HALF_TURN_SPAN = 0.5


def fit_half_angle():
    nodes = np.cos((np.arange(400) + 0.5) * np.pi / 400) * HALF_TURN_SPAN
    square = nodes * nodes
    root = math.sqrt(2.0)
    odd = np.stack([nodes * square**i for i in range(5)], 1)
    even = np.stack([square**i for i in range(5)], 1)
    sin_fit = np.linalg.lstsq(odd, root * np.sin(np.pi * nodes), rcond=None)[0]
    cos_fit = np.linalg.lstsq(even, root * np.cos(np.pi * nodes), rcond=None)[0]
    return [float(v) for v in sin_fit], [float(v) for v in cos_fit]


SIN_FIT, COS_FIT = fit_half_angle()


def horner(square, coefs):
    value = coefs[-1] * square + coefs[-2]
    for coef in coefs[-3::-1]:
        value = value * square + coef
    return value


def split(value):
    high = value.astype(jnp.bfloat16)
    return high, (value - high.astype(jnp.float32)).astype(jnp.bfloat16)


def cos_sin_turns(turns):
    magic = 12582912.0
    rest = turns - ((turns + magic) - magic)
    square = rest * rest
    s = rest * horner(square, SIN_FIT)
    c = horner(square, COS_FIT)
    return 1.0 - s * s, s * c


def dot(a, b, dims):
    return lax.dot_general(a, b, (dims, ((), ())), preferred_element_type=jnp.float32)


NN = ((1,), (0,))
TN = ((0,), (0,))


def coordinate_parts(coords):
    high = coords.astype(jnp.bfloat16).astype(jnp.float32)
    rest = coords - high
    mid = rest.astype(jnp.bfloat16).astype(jnp.float32)
    low = rest - mid
    return jnp.concatenate([high, mid, low, jnp.zeros_like(low)], axis=0).astype(jnp.bfloat16)


MESH = pl.DeviceIdType.MESH


def run_tiles(lo, hi, step, body_at):
    def trip(t, _):
        body_at(pl.multiple_of(t * step, step))
        return 0

    lax.fori_loop(lo // step, hi // step, trip, 0)


def partner_of(me, bit):
    b = lax.rem(lax.div(me, 1 << bit), 2)
    return b, me + (1 - 2 * b) * (1 << bit)


def sum_steps(me, order, part, full, recv, send_sems, recv_sems):
    lo, n, at, sem = 0, part.shape[0], 0, 0
    for bit in order:
        b, other = partner_of(me, bit)
        half = n // 2
        gone = pl.multiple_of(lo + (1 - b) * half, 8)
        kept = pl.multiple_of(lo + b * half, 8)
        copy = pltpu.make_async_remote_copy(
            part.at[pl.ds(gone, half)], recv.at[pl.ds(at, half)],
            send_sems.at[sem], recv_sems.at[sem],
            device_id={"slab": other}, device_id_type=MESH,
        )
        copy.start()
        yield
        copy.wait()
        part[pl.ds(kept, half), :] += recv[at : at + half, :]
        lo, n, at, sem = kept, half, at + half, sem + 1
    full[pl.ds(lo, n), :] = part[pl.ds(lo, n), :]
    for bit in order[::-1]:
        b, other = partner_of(me, bit)
        rows = pl.ds(pl.multiple_of(lo, 8), n)
        copy = pltpu.make_async_remote_copy(
            full.at[rows], full.at[rows],
            send_sems.at[sem], recv_sems.at[sem],
            device_id={"slab": other}, device_id_type=MESH,
        )
        copy.start()
        yield
        copy.wait()
        lo, n, sem = lo - b * n, n * 2, sem + 1


def small_steps(me, bits, part, recv, send_sems, recv_sems):
    for bit in range(bits):
        _, other = partner_of(me, bit)
        copy = pltpu.make_async_remote_copy(
            part.at[bit], recv.at[bit], send_sems.at[bit], recv_sems.at[bit],
            device_id={"slab": other}, device_id_type=MESH,
        )
        copy.start()
        yield
        copy.wait()
        part[bit + 1] = part[bit] + recv[bit]


def advance(*steps):
    live = False
    for one in steps:
        live = next(one, "end") != "end" or live
    return live


def times_split(a, matrix):
    c = matrix.shape[1]
    m_high, m_low = split(matrix)
    a_high, a_low = split(a)
    both = dot(a_high, jnp.concatenate([m_high, m_low], 1), NN)
    return both[:, :c] + both[:, c:] + dot(a_low, m_high, NN)


def ewald_kernel(
    bits, tally, states, coords, k_parts, kernels, first_matrix, second_matrix, out,
    high, low, lhs, sums, density, charge, w, fresh, potential,
    part, full, recv, small, small_recv, s_send, s_recv, x_send, x_recv,
):
    me = lax.axis_index("slab")
    slots, c = states.shape
    kh = part.shape[2] // 2
    wide = 2 * kh

    barrier = pltpu.get_barrier_semaphore()
    for bit in range(bits):
        pl.semaphore_signal(barrier, inc=1, device_id={"slab": partner_of(me, bit)[1]}, device_id_type=MESH)
    pl.semaphore_wait(barrier, bits)

    orders = [list(range(bits)), [0] + list(range(2, bits)) + [1]]

    def big(layer, half):
        return sum_steps(
            me, orders[half], part.at[layer, half], full.at[layer, half], recv.at[layer, half],
            s_send.at[layer, half], s_recv.at[layer, half],
        )

    def little(layer):
        return small_steps(me, bits, small.at[layer], small_recv.at[layer], x_send.at[layer], x_recv.at[layer])

    def occ_column(at):
        rows = at + lax.broadcasted_iota(jnp.int32, (TILE, c), 0)
        return (rows < tally[0]).astype(jnp.float32)

    def place_lhs(at, masked):
        flipped = masked.T
        x_high, x_low = split(flipped)
        lhs[:c, pl.ds(at, TILE)] = x_high
        lhs[c : 2 * c, pl.ds(at, TILE)] = x_low

    def phases(half, at):
        columns = coordinate_parts(coords[:, pl.ds(at, TILE)])
        step = 256
        for k in range(0, kh, step):
            turns = dot(columns, k_parts[:, half * kh + k : half * kh + k + step], TN)
            for value, to in zip(cos_sin_turns(turns), (k, kh + k)):
                v_high, v_low = split(value)
                high[half, pl.ds(at, TILE), to : to + step] = v_high
                low[half, pl.ds(at, TILE), to : to + step] = v_low

    def gather_sums(half, at, with_density):
        rows = 2 * c + (16 if with_density else 0)
        one = dot(lhs[:rows, pl.ds(at, TILE)], high[half, pl.ds(at, TILE), :], NN)
        two = dot(lhs[:c, pl.ds(at, TILE)], low[half, pl.ds(at, TILE), :], NN)
        sums[half] += one[:c] + one[c : 2 * c] + two
        if with_density:
            three = dot(lhs[2 * c :, pl.ds(at, TILE)], low[half, pl.ds(at, TILE), :], NN)
            density[half] += (one[2 * c :] + three)[:8]

    def first_pass(half):
        def body_at(at):
            if half == 0:
                masked = states[pl.ds(at, TILE), :] * occ_column(at)
                place_lhs(at, masked)
                charge[...] += jnp.broadcast_to(jnp.sum(masked, axis=0, keepdims=True), (8, c))
                lane = at + lax.broadcasted_iota(jnp.int32, (16, TILE), 1)
                lhs[2 * c :, pl.ds(at, TILE)] = (lane < tally[0]).astype(jnp.float32).astype(jnp.bfloat16)
            phases(half, at)
            gather_sums(half, at, True)

        return body_at

    def finish_sums(layer, half):
        for k in range(0, wide, c):
            part[layer, half, k : k + c, :] = sums[half, :, k : k + c].T

    def place_small(layer):
        if layer == 0:
            for half in range(2):
                for i in range(wide // c):
                    small[0, 0, half * (wide // c) + i : half * (wide // c) + i + 1, :] = density[
                        half, :1, i * c : (i + 1) * c
                    ]
        else:
            small[1, 0, : 2 * wide // c, :] = jnp.zeros((2 * wide // c, c), jnp.float32)
        base = 2 * wide // c
        small[layer, 0, base : base + 8, :] = charge[...]
        small[layer, 0, base + 8 : base + 16, :] = jnp.full((8, c), tally[0], jnp.int32).astype(jnp.float32)

    def weigh(layer, half):
        base = 2 * wide // c
        mean = small[layer, bits, base : base + 1, :] / small[layer, bits, base + 8 : base + 9, :]
        root = jnp.sqrt(small[layer, bits, base + 8 : base + 9, :])
        for i in range(wide // c):
            row = half * (wide // c) + i
            dens = jnp.broadcast_to(small[0, bits, row : row + 1, :], (c, c)).T
            k = half * kh + (i * c) % kh
            value = (full[layer, half, i * c : (i + 1) * c, :] - dens * mean) / root
            v_high, v_low = split(value * kernels[layer, k : k + c, :])
            w[half, i * c : (i + 1) * c, :c] = v_high
            w[half, i * c : (i + 1) * c, c:] = v_low

    def potential_at(half, at):
        both = dot(high[half, pl.ds(at, TILE), :], w[half], NN)
        return both[:, :c] + both[:, c:] + dot(low[half, pl.ds(at, TILE), :], w[half, :, :c], NN)

    def updated(layer, source, at):
        value = potential[pl.ds(at, TILE), :] + potential_at(1, at)
        v = times_split(value, first_matrix[layer])
        return source[pl.ds(at, TILE), :] + times_split(v / (1.0 + jnp.exp(-v)), second_matrix[layer])

    def keep_potential(at):
        potential[pl.ds(at, TILE), :] = potential_at(0, at)

    def middle(at):
        value = updated(0, states, at)
        fresh[pl.ds(at, TILE), :] = value
        masked = value * occ_column(at)
        place_lhs(at, masked)
        charge[...] += jnp.broadcast_to(jnp.sum(masked, axis=0, keepdims=True), (8, c))
        gather_sums(0, at, False)

    def last(at):
        out[pl.ds(at, TILE), :] = updated(1, fresh, at) * occ_column(at)

    def during(steps, pieces, body_at):
        step = slots // pieces
        for i in range(pieces):
            run_tiles(i * step, (i + 1) * step, TILE, body_at)
            advance(*steps)

    def drain(*steps):
        while advance(*steps):
            pass

    sums[...] = jnp.zeros_like(sums)
    density[...] = jnp.zeros_like(density)
    charge[...] = jnp.zeros_like(charge)
    for layer in range(2):
        if layer == 0:
            run_tiles(0, slots, TILE, first_pass(0))
        else:
            sums[...] = jnp.zeros_like(sums)
            charge[...] = jnp.zeros_like(charge)
            run_tiles(0, slots, TILE, middle)
        finish_sums(layer, 0)
        a = big(layer, 0)
        advance(a)
        during([a], PIECES, first_pass(1) if layer == 0 else lambda at: gather_sums(1, at, False))
        finish_sums(layer, 1)
        place_small(layer)
        b, x = big(layer, 1), little(layer)
        drain_first(a, b, x)
        weigh(layer, 0)
        during([b], PIECES, keep_potential)
        drain(b)
        weigh(layer, 1)
    run_tiles(0, slots, TILE, last)


def drain_first(a, b, x):
    while True:
        live = [next(one, "end") != "end" for one in (a, x)]
        next(b, "end")
        if not any(live):
            return


def body(states, coords, tallies, lattice, kernels, first_matrix, second_matrix):
    slots, c = states.shape
    kspace = lattice.shape[1]
    bits = lax.axis_size("slab").bit_length() - 1
    f32, b16 = jnp.float32, jnp.bfloat16
    coords8 = jnp.pad(coords, ((0, 5), (0, 0)))
    k8 = jnp.pad(lattice, ((0, 5), (0, 0))).astype(b16)
    k_parts = jnp.concatenate([k8, k8, k8, k8], 0)
    vmem = pl.BlockSpec(memory_space=pltpu.VMEM)
    extra = 2 * kspace // c + 16
    return pl.pallas_call(
        functools.partial(ewald_kernel, bits),
        in_specs=[pl.BlockSpec(memory_space=pltpu.SMEM)] + [vmem] * 6,
        out_specs=vmem,
        out_shape=jax.ShapeDtypeStruct((slots, c), f32),
        scratch_shapes=[
            pltpu.VMEM((2, slots, kspace), b16),
            pltpu.VMEM((2, slots, kspace), b16),
            pltpu.VMEM((2 * c + 16, slots), b16),
            pltpu.VMEM((2, c, kspace), f32),
            pltpu.VMEM((2, 8, kspace), f32),
            pltpu.VMEM((8, c), f32),
            pltpu.VMEM((2, kspace, 2 * c), b16),
            pltpu.VMEM((slots, c), f32),
            pltpu.VMEM((slots, c), f32),
            pltpu.VMEM((2, 2, kspace, c), f32),
            pltpu.VMEM((2, 2, kspace, c), f32),
            pltpu.VMEM((2, 2, kspace, c), f32),
            pltpu.VMEM((2, bits + 1, extra, c), f32),
            pltpu.VMEM((2, bits, extra, c), f32),
            pltpu.SemaphoreType.DMA((2, 2, 2 * bits)),
            pltpu.SemaphoreType.DMA((2, 2, 2 * bits)),
            pltpu.SemaphoreType.DMA((2, bits)),
            pltpu.SemaphoreType.DMA((2, bits)),
        ],
        compiler_params=pltpu.CompilerParams(
            vmem_limit_bytes=62 * 2**20, collective_id=0, has_side_effects=True
        ),
    )(tallies, states, coords8, k_parts, kernels, first_matrix, second_matrix)


def solution(mesh):
    in_specs = (
        P(("groups", "slab"), None),
        P(None, ("groups", "slab")),
        P(("groups", "slab")),
        P(),
        P(),
        P(),
        P(),
    )
    out_specs = P(("groups", "slab"), None)
    return jax.shard_map(body, mesh=mesh, in_specs=in_specs, out_specs=out_specs, check_vma=False)
```

time: 302 us -> 126 us (0.42)
  blocking collectives: 125 us -> 0 us
  waiting for transfers between devices: 59.3 us -> 0 us
  Pallas kernels: 89.6 us -> 120 us
  between operations: 14.8 us -> 0.66 us
  other arithmetic: 9.23 us -> 1.35 us
    psum x2 -> x0, blocking collectives: 125 us -> none  [the longest x1 65.7 us: body(): lax.psum((s, density[:1], charge[:, :1], total), 'slab')]
    psum x2 -> x0, waiting for transfers between devices: 59.2 us -> none  [the longest x1 32.5 us: body(): s, charge = lax.psum((s, charge[:, :1]), 'slab')]
    pallas_call x3 -> x1, Pallas kernels: 89.6 us -> 120 us  [body(): pl.pallas_call(functools.partial(ewald_kernel, bits), in_specs=[pl.BlockS...]
    convert_element_type x4 -> x0, other arithmetic: 6.41 us -> none  [weights(): return (w_high.astype(b16), (w - w_high).astype(b16))]
  transfers between devices with their start and end apart: 2 -> 0, of which waited for: 2 -> 0; matrix products, arithmetic and copies ran while one was open for 1% -> 0% of each run, Pallas kernels for 0% -> 0%
where the time goes in v1:
time: 126 us
  Pallas kernels  120 us (95%)
  local copies, waits for them, and re-layouts  4.11 us (3%)
  other arithmetic  1.35 us (1%)
    pallas_call x1, Pallas kernels, body(): pl.pallas_call(functools.partial(ewald_kernel, bits), in_specs=[pl.BlockS...  120 us
    unnamed x1, local copies, waits for them, and re-layouts  2.65 us

profile of v1, /device:TPU:0, one launch (start us, length us, event | category | flops | bytes accessed | tf_op | source)
XLA Modules:
  0.0 126.1 jit_solution(13222873489297880374)
XLA Ops:
  0.7 0.7 convert.4
  1.4 0.6 pad_maximum_fusion.k_parts
  2.0 1.4 %pad.9.coords = f32[8,3072]{1,0:T(8,128)} pad(f32[3,3072]{1,0:T(4,128)} %param.8, f32[]{:T(128)} %constant.3.clone.1), padding=0_5x0_0 | pad | bytes 135172 | tf_op jit(solution)/shard_map/jit(_pad)/pad | solution.py:313
  3.5 120.0 %shard_map.73 = f32[3072,128]{1,0:T(8,128)} custom-call(s32[1]{0:T(128)S(6)} %copy.9.tally, f32[3072,128]{1,0:T(8,128)} %states.1, f32[8,3072]{1,0:T(8,128)} %pad.9.coords, bf16[32,1024]{1,0:T(8,128)(2,1)} %pad_maximum_fusion.k_parts, f32[2,1024,128]{2,1,0:T(8,128)} %kernels.1, f32[2,128,128]{2,1,0:T(8,128)} %first_matrix.1, f32[2,128,128]{2,1,0:T(8,128)} %second_matrix.1), custom_call_target="tpu_custom_call" | custom-call | tf_op jit(solution)/shard_map/pallas_call | solution.py:318
  123.4 2.7 %copy.10 = f32[3072,128]{1,0:T(8,128)} copy(f32[3072,128]{1,0:T(8,128)} %shard_map.73) | data formatting | bytes 3145728
  (1 shorter events, 0.0 us)
